TPU v7x, 32 devices: a whole 2x2x4 slice. The times are simulated.
32 devices in a mesh: grp: 4 (over y, x), dev: 8 (over z, core).
Axes of the slice: x: 2, y: 2, z: 4, core: 2. Of those that a mesh axis runs over, the one named last changes fastest.
Arguments:
- features: bfloat16 [2048, 32, 512], P(('grp', 'dev')), may hold values from -6 to 6
- occupancy: int32 [2048, 512], P(('grp', 'dev')), may hold values 0 or 1
- neighbours: int32 [2048, 27], P(('grp', 'dev')), may hold values from -1 to 2047, as said below
- conv_weight: bfloat16 [32, 32, 3, 3, 3], replicated, may hold values from -0.21875 to 0.21875
- conv_bias: float32 [32], replicated, may hold values from -3 to 3
- point_brick: int32 [262144], P(('grp', 'dev')), may hold values from 0 to 2047, as said below
- point_cell: int32 [262144], P(('grp', 'dev')), may hold values from 0 to 438, as said below
- point_frac: float32 [3, 262144], P(None, ('grp', 'dev')), may hold values from 0 to 1
- decoder_in: bfloat16 [64, 32], replicated, may hold values from -1 to 1
- decoder_bias: float32 [64], replicated, may hold values from -3 to 3
- decoder_out: bfloat16 [64], replicated, may hold values from -0.75 to 0.75
Outputs:
- block_out: bfloat16 [2048, 32, 512], P(('grp', 'dev'))
- point_value: float32 [262144], P(('grp', 'dev'))
Inputs may be any that keep to these rules, and one draw needn't show every extreme that they name: `neighbours`: entry 9 (dx + 1) + 3 (dy + 1) + (dz + 1) of a brick's list names the brick displaced by (dx, dy, dz) bricks, or -1 if there is none. Bricks are numbered device by device in the order of grp then dev, 64 to a device. A brick named at dx = -1 lies on the previous device, at dx = 0 on the brick's own device, at dx = +1 on the next device. The relation is symmetric and entry 13 is the brick itself. `point_brick`: the point rows of one device name bricks of any one device at most 512 times, and some device's bricks are named exactly 512 times by the rows of every device. `point_cell`: 64 x + 8 y + z of the lower corner (x, y, z) of the cell that holds the point, each of x, y, z from 0 to 6.
All inputs are finite; a program needn't handle non-finite values. No bound on the sum of `occupancy` on one device may be relied on, other than what follows from the above.
Results may differ from a plain program's by a relative error of at most 0.0044.
Values may be sent and summed in bfloat16 or wider, within the bound.
A program may use at most 128 MiB of HBM per device.

v0:
```python
import math

import jax
import jax.numpy as jnp
from jax import lax
from jax.sharding import PartitionSpec as P


def from_behind(value, axis, steps):
    count = lax.axis_size(axis)
    initial, last = (max(0, -steps), min(count, count - steps))
    return lax.ppermute(value, axis, [(source, source + steps) for source in range(initial, last)])


def span_of(direction):
    if direction < 0:
        return (7, 8)
    if direction > 0:
        return (0, 1)
    return (0, 8)


def target_of(direction):
    if direction < 0:
        return (0, 1)
    if direction > 0:
        return (9, 10)
    return (1, 9)


def take_slab(source5, listed, first_id, x_range, y_range, z_range):
    slab = source5[:, :, x_range[0] : x_range[1], y_range[0] : y_range[1], z_range[0] : z_range[1]]
    present = listed >= 0
    safe_rows = jnp.clip(listed - first_id, 0, slab.shape[0] - 1)
    taken = jnp.take(slab, safe_rows, axis=0)
    return taken * present[:, None, None, None, None].astype(taken.dtype)


def trilinear_rows(row_table, base_column, fraction):
    summed = jnp.zeros((base_column.shape[0], row_table.shape[1]), jnp.float32)
    for corner in range(8):
        corner_bits = [corner >> 2 & 1, corner >> 1 & 1, corner & 1]
        weight = jnp.ones_like(fraction[0])
        for axis_id in range(3):
            weight = weight * (
                fraction[axis_id] if corner_bits[axis_id] else 1.0 - fraction[axis_id]
            )
        column = base_column + corner_bits[0] * 64 + corner_bits[1] * 8 + corner_bits[2]
        summed = summed + weight[:, None] * jnp.take(row_table, column, axis=0).astype(jnp.float32)
    return summed


def decoder_rows(sample, decoder_in, decoder_bias, decoder_out):
    hidden = jax.nn.relu(
        jnp.einsum(
            "nc,hc->nh", sample.astype(jnp.bfloat16), decoder_in, preferred_element_type=jnp.float32
        )
        + decoder_bias[None, :]
    ).astype(jnp.bfloat16)
    return jnp.dot(hidden, decoder_out[:, None], preferred_element_type=jnp.float32)[:, 0]


def per_device(
    features,
    occupancy,
    neighbours,
    conv_weight,
    conv_bias,
    point_brick,
    point_cell,
    point_frac,
    decoder_in,
    decoder_bias,
    decoder_out,
):
    brick_count = features.shape[0]
    channels = features.shape[1]
    my_index = lax.axis_index(("grp", "dev"))
    masked = features * occupancy[:, None, :].astype(features.dtype)
    own_grid = masked.reshape(brick_count, channels, 8, 8, 8)
    previous = from_behind(masked[:, :, 448:], ("grp", "dev"), 1)
    following = from_behind(masked[:, :, :64], ("grp", "dev"), -1)
    previous_grid = previous.reshape(brick_count, channels, 1, 8, 8)
    following_grid = following.reshape(brick_count, channels, 1, 8, 8)
    previous_x = (0, 1)
    padded = jnp.pad(own_grid, ((0, 0), (0, 0), (1, 1), (1, 1), (1, 1)))
    for step_x in (-1, 0, 1):
        if step_x < 0:
            source5, first_id, x_range = (previous_grid, (my_index - 1) * brick_count, previous_x)
        elif step_x > 0:
            source5, first_id, x_range = (following_grid, (my_index + 1) * brick_count, (0, 1))
        else:
            source5, first_id, x_range = (own_grid, my_index * brick_count, (0, 8))
        for step_y in (-1, 0, 1):
            for step_z in (-1, 0, 1):
                if step_x == 0 and step_y == 0 and (step_z == 0):
                    continue
                neighbour_slot = 9 * (step_x + 1) + 3 * (step_y + 1) + (step_z + 1)
                slab = take_slab(
                    source5,
                    neighbours[:, neighbour_slot],
                    first_id,
                    x_range,
                    span_of(step_y),
                    span_of(step_z),
                )
                tx, ty, tz = (target_of(step_x), target_of(step_y), target_of(step_z))
                padded = padded.at[:, :, tx[0] : tx[1], ty[0] : ty[1], tz[0] : tz[1]].set(slab)
    convolved = lax.conv_general_dilated(
        padded,
        conv_weight,
        (1, 1, 1),
        "VALID",
        dimension_numbers=("NCDHW", "OIDHW", "NCDHW"),
        preferred_element_type=jnp.float32,
    ).reshape(brick_count, channels, 512)
    occupied = occupancy[:, None, :].astype(jnp.float32)
    block_out = (
        masked.astype(jnp.float32) + occupied * jax.nn.relu(convolved + conv_bias[None, :, None])
    ).astype(jnp.bfloat16)
    device_total = lax.axis_size(("grp", "dev"))
    point_count = point_brick.shape[0]
    capacity = 2 * point_count // device_total
    owner_dev = point_brick // brick_count
    local_brick = point_brick - owner_dev * brick_count
    block_rows = math.gcd(point_count, 512)
    block_total = point_count // block_rows
    dest_hits = (
        (owner_dev[:, None] == jnp.arange(device_total, dtype=jnp.int32)[None, :])
        .astype(jnp.bfloat16)
        .reshape(block_total, block_rows, device_total)
    )
    lower_tri = (jnp.arange(block_rows)[:, None] > jnp.arange(block_rows)[None, :]).astype(
        jnp.bfloat16
    )
    within = jnp.einsum("ij,bjd->bid", lower_tri, dest_hits, preferred_element_type=jnp.float32)
    hits_float = dest_hits.astype(jnp.float32)
    block_sums = jnp.sum(hits_float, axis=1)
    offsets = jnp.cumsum(block_sums, axis=0) - block_sums
    slot_index = (
        jnp.sum((within + offsets[:, None, :]) * hits_float, axis=2)
        .reshape(point_count)
        .astype(jnp.int32)
    )
    requests = (
        jnp.full((device_total, 2, capacity), -1, jnp.int32)
        .at[owner_dev, :, slot_index]
        .set(jnp.stack([local_brick, point_cell], axis=1))
    )
    fractions = (
        jnp.zeros((device_total, 3, capacity), jnp.float32)
        .at[owner_dev, :, slot_index]
        .set(point_frac.T)
    )
    row_table = jnp.transpose(block_out, (0, 2, 1)).reshape(brick_count * 512, channels)
    request_part = lax.all_to_all(requests, ("grp", "dev"), split_axis=0, concat_axis=0, tiled=True)
    brick_ids = request_part[:, 0, :].reshape(-1)
    live_slot = brick_ids >= 0
    base_column = jnp.where(live_slot, brick_ids * 512 + request_part[:, 1, :].reshape(-1), 0)
    fraction_rows = jnp.transpose(
        lax.all_to_all(fractions, ("grp", "dev"), split_axis=0, concat_axis=0, tiled=True),
        (1, 0, 2),
    ).reshape(3, -1)
    values = decoder_rows(
        trilinear_rows(row_table, base_column, fraction_rows), decoder_in, decoder_bias, decoder_out
    )
    returned = lax.all_to_all(
        jnp.where(live_slot, values, 0.0).reshape(request_part.shape[0], -1),
        ("grp", "dev"),
        split_axis=0,
        concat_axis=0,
        tiled=True,
    )
    point_value = returned[owner_dev, slot_index]
    return (block_out, point_value)


def solution(mesh):
    return jax.shard_map(
        per_device,
        mesh=mesh,
        in_specs=(
            P(("grp", "dev"), None, None),
            P(("grp", "dev"), None),
            P(("grp", "dev"), None),
            P(),
            P(),
            P(("grp", "dev")),
            P(("grp", "dev")),
            P(None, ("grp", "dev")),
            P(),
            P(),
            P(),
        ),
        out_specs=(P(("grp", "dev"), None, None), P(("grp", "dev"))),
        check_vma=False,
    )
```

profile of v0, /device:TPU:0, one launch (start us, length us, event | category | flops | bytes accessed | tf_op | source)
XLA Modules:
  0.0 1047.2 jit_solution(4940997256610368631)
XLA Ops:
  1.8 5.3 copy.210
  22.8 24.7 %scatter_custom_fusion = s32[16384,2]{1,0:T(8,128)} fusion(s32[8192]{0:T(1024)S(1)} %broadcast_select_fusion, s32[8192,2]{1,0:T(8,128)} %copy.278, s32[]{:T(128)} %constant.985.clone.1), kind=kCustom, calls=%fused_computation.49 | custom fusion | bytes 131584
  47.5 5.9 copy.279
  53.3 10.0 all-to-all-start
  68.9 6.3 fusion.96
  121.6 24.7 %scatter_custom_fusion.1 = f32[3,16384]{0,1:T(8,128)} fusion(s32[8192]{0:T(1024)S(1)} %broadcast_select_fusion, f32[8192,3]{1,0:T(8,128)} %copy.281, f32[]{:T(128)} %constant.990.clone.1), kind=kCustom, calls=%fused_computation.47 | custom fusion | bytes 197120
  146.2 5.9 copy.282
  152.2 8.9 pad.108
  162.2 6.5 all-to-all-start.1
  231.3 8.0 scatter.106
  253.0 7.9 scatter.116
  265.4 26.8 %scatter.120 = bf16[64,32,10,10,10]{0,4,3,2,1:T(8,128)(2,1)} dynamic-update-slice(bf16[64,32,10,10,10]{0,4,3,2,1:T(8,128)(2,1)} %scatter.119, bf16[64,32,8,8,1]{0,4,3,2,1:T(2,128)(2,1)S(1)} %copy-done.5, s32[]{:T(128)} %constant.981.clone.1, s32[]{:T(128)} %constant.981.clone.1, s32[]{:T(128)} %constant.988.clone.1, s32[]{:T(128)} %constant.988.clone.1, s32[]{:T(128)} %constant.981.clone.1) | dynamic-update-slice | bytes 524292 | tf_op jit(solution)/shard_map/scatter | solution.py:108
  292.2 26.8 %scatter.121 = bf16[64,32,10,10,10]{0,4,3,2,1:T(8,128)(2,1)} dynamic-update-slice(bf16[64,32,10,10,10]{0,4,3,2,1:T(8,128)(2,1)} %scatter.120, bf16[64,32,8,8,1]{0,4,3,2,1:T(2,128)(2,1)S(1)} %copy.246, s32[]{:T(128)} %constant.981.clone.1, s32[]{:T(128)} %constant.981.clone.1, s32[]{:T(128)} %constant.988.clone.1, s32[]{:T(128)} %constant.988.clone.1, s32[]{:T(128)} %constant.989.clone.1) | dynamic-update-slice | bytes 524292 | tf_op jit(solution)/shard_map/scatter | solution.py:108
  323.6 7.7 scatter.125
  345.9 7.7 scatter.135
  362.8 21.9 %fusion.6 = f32[64,32,8,8,8]{0,1,4,3,2:T(8,128)S(1)} fusion(bf16[32,32,3,3,3]{1,0,4,3,2:T(8,128)(2,1)S(1)} %copy-done, bf16[64,32,10,10,10]{0,4,3,2,1:T(8,128)(2,1)} %scatter.169), kind=kOutput, calls=%fused_computation.45 | convolution fusion | flops 1811939328 | bytes 8345600 | tf_op jit(solution)/shard_map/conv_general_dilated | solution.py:109
  384.7 10.5 %fusion.5 = bf16[64,32,512]{0,2,1:T(8,128)(2,1)} fusion(f32[64,32,512]{0,1,2:T(8,128)S(1)} %bitcast.347, f32[32]{0:T(128)S(1)} %copy-done.61, f32[64,512]{0,1:T(8,128)S(1)} %copy-done.14, bf16[64,32,512]{0,2,1:T(8,128)(2,1)S(1)} %copy-done.4, bf16[64,512]{0,1:T(8,128)(2,1)S(1)} %copy-done.13), kind=kLoop, calls=%fused_computation.44 | loop fusion | flops 7340032 | bytes 8585344 | tf_op jit(solution)/shard_map/convert_element_type | solution.py:120
  395.2 16.2 %copy.284 = bf16[64,512,32]{2,1,0:T(8,128)(2,1)} copy(bf16[64,512,32]{0,1,2:T(8,128)(2,1)} %bitcast.342) | data formatting | bytes 4194304 | tf_op jit(solution)/shard_map/transpose | solution.py:155
  411.5 59.9 %gather_fusion.34 = bf16[16384,32]{1,0:T(8,128)(2,1)} fusion(bf16[32768,32]{1,0:T(8,128)(2,1)} %bitcast.329, s32[16384]{0:T(1024)S(1)} %copy-done.32), kind=kCustom, calls=%fused_computation.33.clone | custom fusion | bytes 2162688 | tf_op jit(solution)/shard_map/jit(_take)/gather | solution.py:49
  474.8 59.9 %gather_fusion.33 = bf16[16384,32]{1,0:T(8,128)(2,1)} fusion(bf16[32768,32]{1,0:T(8,128)(2,1)} %bitcast.330, s32[16384]{0:T(1024)S(1)} %copy-done.31), kind=kCustom, calls=%fused_computation.32.clone | custom fusion | bytes 2162688 | tf_op jit(solution)/shard_map/jit(_take)/gather | solution.py:49
  538.2 59.9 %gather_fusion.32 = bf16[16384,32]{1,0:T(8,128)(2,1)} fusion(bf16[32768,32]{1,0:T(8,128)(2,1)} %bitcast.331, s32[16384]{0:T(1024)S(1)} %copy-done.30), kind=kCustom, calls=%fused_computation.31.clone | custom fusion | bytes 2162688 | tf_op jit(solution)/shard_map/jit(_take)/gather | solution.py:49
  601.6 59.9 %gather_fusion.31 = bf16[16384,32]{1,0:T(8,128)(2,1)} fusion(bf16[32768,32]{1,0:T(8,128)(2,1)} %bitcast.332, s32[16384]{0:T(1024)S(1)} %copy-done.29), kind=kCustom, calls=%fused_computation.30.clone | custom fusion | bytes 2162688 | tf_op jit(solution)/shard_map/jit(_take)/gather | solution.py:49
  666.1 59.9 %gather_fusion.30 = bf16[16384,32]{1,0:T(8,128)(2,1)} fusion(bf16[32768,32]{1,0:T(8,128)(2,1)} %bitcast.333, s32[16384]{0:T(1024)S(1)} %copy-done.28), kind=kCustom, calls=%fused_computation.29.clone | custom fusion | bytes 2162688 | tf_op jit(solution)/shard_map/jit(_take)/gather | solution.py:49
  730.6 59.9 %gather_fusion.29 = bf16[16384,32]{1,0:T(8,128)(2,1)} fusion(bf16[32768,32]{1,0:T(8,128)(2,1)} %bitcast.334, s32[16384]{0:T(1024)S(1)} %copy-done.27), kind=kCustom, calls=%fused_computation.28.clone | custom fusion | bytes 2162688 | tf_op jit(solution)/shard_map/jit(_take)/gather | solution.py:49
  795.1 59.9 %gather_fusion.28 = bf16[16384,32]{1,0:T(8,128)(2,1)} fusion(bf16[32768,32]{1,0:T(8,128)(2,1)} %bitcast.335, s32[16384]{0:T(1024)S(1)} %copy-done.26), kind=kCustom, calls=%fused_computation.27.clone | custom fusion | bytes 2162688 | tf_op jit(solution)/shard_map/jit(_take)/gather | solution.py:49
  854.9 59.9 %gather_fusion.27 = bf16[16384,32]{1,0:T(8,128)(2,1)} fusion(bf16[32768,32]{1,0:T(8,128)(2,1)} %bitcast.336, s32[16384]{0:T(1024)S(1)} %copy-done.25), kind=kCustom, calls=%fused_computation.7.clone | custom fusion | bytes 2162688 | tf_op jit(solution)/shard_map/jit(_take)/gather | solution.py:49
  914.8 4.8 copy.285
  919.6 4.7 copy.286
  926.6 6.5 fusion.12
  933.8 5.7 all-to-all-start.2
  939.5 5.6 copy.294
  946.9 100.1 %gather_fusion = f32[8192]{0:T(1024)} fusion(f32[32,512]{1,0:T(8,128)S(1)} %bitcast.328, s32[8192]{0:T(1024)S(1)} %bitcast.337), kind=kCustom, calls=%fused_computation.34 | custom fusion | bytes 131072 | tf_op jit(solution)/shard_map/gather | solution.py:174
  (340 shorter events, 207.3 us)
Async XLA Ops:
  0.6 362.1 %copy-start = (bf16[32,32,3,3,3]{1,0,4,3,2:T(8,128)(2,1)S(1)}, bf16[32,32,3,3,3]{1,0,4,3,2:T(8,128)(2,1)}, u32[]{:S(2)}) copy-start(bf16[32,32,3,3,3]{1,0,4,3,2:T(8,128)(2,1)} %param.82) | copy-start | bytes 165892
  12.8 161.6 %collective-permute-start.1 = (bf16[64,32,64]{0,2,1:T(8,128)(2,1)}, bf16[64,32,64]{0,2,1:T(8,128)(2,1)}, u32[]{:S(2)}, u32[]{:S(2)}) collective-permute-start(bf16[64,32,64]{0,2,1:T(8,128)(2,1)} %get-tuple-element.382), channel_id=1, source_target_pairs={{1,0},{2,1},{3,2},{4,3},{5,4},{6,5},{7,6},{8,7},{9,8},{10,9},{11,1... | collective-permute-start | bytes 786440 | tf_op jit(solution)/shard_map/ppermute | solution.py:12
  14.1 157.1 %collective-permute-start = (bf16[64,32,64]{0,2,1:T(8,128)(2,1)}, bf16[64,32,64]{0,2,1:T(8,128)(2,1)}, u32[]{:S(2)}, u32[]{:S(2)}) collective-permute-start(bf16[64,32,64]{0,2,1:T(8,128)(2,1)} %get-tuple-element.383), channel_id=1, source_target_pairs={{0,1},{1,2},{2,3},{3,4},{4,5},{5,6},{6,7},{7,8},{8,9},{9,10},{10,1... | collective-permute-start | bytes 786440 | tf_op jit(solution)/shard_map/ppermute | solution.py:12
  47.4 15.9 %copy-start.36 = (s32[64,27]{0,1:T(8,128)S(1)}, s32[64,27]{0,1:T(8,128)}, u32[]{:S(2)}) copy-start(s32[64,27]{0,1:T(8,128)} %param.81) | copy-start | bytes 20740
  53.3 108.9 %all-to-all-start = ((s32[32,2,512]{2,1,0:T(2,128)}), s32[32,2,512]{2,1,0:T(2,128)S(1)}, u32[]{:S(2)}, u32[]{:S(2)}) async-start(s32[32,2,512]{2,1,0:T(2,128)} %bitcast.116), calls=%async_computation | async-start | bytes 262144 | tf_op jit(solution)/shard_map/all_to_all | solution.py:156
  162.2 762.1 %all-to-all-start.1 = ((f32[32,3,512]{2,1,0:T(4,128)}), f32[32,3,512]{2,1,0:T(4,128)}, u32[]{:S(2)}, u32[]{:S(2)}) async-start(f32[32,3,512]{2,1,0:T(4,128)} %bitcast.119), calls=%async_computation.1 | async-start | bytes 524288 | tf_op jit(solution)/shard_map/all_to_all | solution.py:161
  181.2 11.9 %copy-start.45 = (bf16[64]{0:T(256)(128)(2,1)S(1)}, bf16[64]{0:T(256)(128)(2,1)}, u32[]{:S(2)}) copy-start(bf16[64]{0:T(256)(128)(2,1)} %get-tuple-element.448) | copy-start | bytes 388
  181.3 11.9 %copy-start.46 = (bf16[64]{0:T(256)(128)(2,1)S(1)}, bf16[64]{0:T(256)(128)(2,1)}, u32[]{:S(2)}) copy-start(bf16[64]{0:T(256)(128)(2,1)} %get-tuple-element.450) | copy-start | bytes 388
  181.3 11.9 %copy-start.49 = (pred[64]{0:T(512)(128)(4,1)S(1)}, pred[64]{0:T(512)(128)(4,1)}, u32[]{:S(2)}) copy-start(pred[64]{0:T(512)(128)(4,1)} %get-tuple-element.485) | copy-start | bytes 196
  198.5 15.6 %copy-start.22 = (bf16[64,32,8]{1,0,2:T(8,128)(2,1)S(1)}, bf16[64,32,8]{1,0,2:T(8,128)(2,1)}, u32[]{:S(2)}) copy-start(bf16[64,32,8]{1,0,2:T(8,128)(2,1)} %get-tuple-element.397) | copy-start | bytes 98308
  200.9 14.9 %copy-start.21 = (bf16[64,32,8]{1,0,2:T(8,128)(2,1)S(1)}, bf16[64,32,8]{1,0,2:T(8,128)(2,1)}, u32[]{:S(2)}) copy-start(bf16[64,32,8]{1,0,2:T(8,128)(2,1)} %get-tuple-element.399) | copy-start | bytes 98308
  200.9 24.4 %copy-start.18 = (bf16[64,32,1,8,1]{0,4,3,2,1:T(2,128)(2,1)S(1)}, bf16[64,32,1,8,1]{0,4,3,2,1:T(2,128)(2,1)}, u32[]{:S(2)}) copy-start(bf16[64,32,1,8,1]{0,4,3,2,1:T(2,128)(2,1)} %copy.221) | copy-start | bytes 98308
  200.9 28.9 %copy-start.6 = (bf16[64,32,8,8]{0,3,2,1:T(8,128)(2,1)S(1)}, bf16[64,32,8,8]{0,3,2,1:T(8,128)(2,1)}, u32[]{:S(2)}) copy-start(bf16[64,32,8,8]{0,3,2,1:T(8,128)(2,1)} %copy.223) | copy-start | bytes 786436
  214.1 51.3 %copy-start.5 = (bf16[64,32,8,8,1]{0,4,3,2,1:T(2,128)(2,1)S(1)}, bf16[64,32,8,8,1]{0,4,3,2,1:T(2,128)(2,1)}, u32[]{:S(2)}) copy-start(bf16[64,32,8,8,1]{0,4,3,2,1:T(2,128)(2,1)} %copy.243) | copy-start | bytes 786436
  231.3 92.3 %copy-start.11 = (bf16[64,32,8,1,8]{0,4,3,2,1:T(8,128)(2,1)S(1)}, bf16[64,32,8,1,8]{0,4,3,2,1:T(8,128)(2,1)}, u32[]{:S(2)}) copy-start(bf16[64,32,8,1,8]{0,4,3,2,1:T(8,128)(2,1)} %get-tuple-element.526) | copy-start | bytes 786436
  231.3 100.0 %copy-start.17 = (bf16[64,32,8,1,1]{0,4,3,2,1:T(2,128)(2,1)S(1)}, bf16[64,32,8,1,1]{0,4,3,2,1:T(2,128)(2,1)}, u32[]{:S(2)}) copy-start(bf16[64,32,8,1,1]{0,4,3,2,1:T(2,128)(2,1)} %copy.254) | copy-start | bytes 98308
  239.3 100.5 %copy-start.35 = (bf16[64,32,1,1,1]{0,4,3,2,1:T(2,128)(2,1)S(1)}, bf16[64,32,1,1,1]{0,4,3,2,1:T(2,128)(2,1)}, u32[]{:S(2)}) copy-start(bf16[64,32,1,1,1]{0,4,3,2,1:T(2,128)(2,1)} %copy.261) | copy-start | bytes 12292
  243.8 102.1 %copy-start.7 = (bf16[64,32,8,8]{0,3,2,1:T(8,128)(2,1)S(1)}, bf16[64,32,8,8]{0,3,2,1:T(8,128)(2,1)}, u32[]{:S(2)}) copy-start(bf16[64,32,8,8]{0,3,2,1:T(8,128)(2,1)} %copy.266) | copy-start | bytes 786436
  243.8 102.1 %copy-start.43 = (bf16[64]{0:T(256)(128)(2,1)S(1)}, bf16[64]{0:T(256)(128)(2,1)}, u32[]{:S(2)}) copy-start(bf16[64]{0:T(256)(128)(2,1)} %get-tuple-element.497) | copy-start | bytes 388
  243.8 102.1 %copy-start.44 = (pred[64]{0:T(512)(128)(4,1)S(1)}, pred[64]{0:T(512)(128)(4,1)}, u32[]{:S(2)}) copy-start(pred[64]{0:T(512)(128)(4,1)} %get-tuple-element.510) | copy-start | bytes 196
  265.4 92.7 %copy-start.34 = (bf16[64,32,1,1,1]{0,4,3,2,1:T(2,128)(2,1)S(1)}, bf16[64,32,1,1,1]{0,4,3,2,1:T(2,128)(2,1)}, u32[]{:S(2)}) copy-start(bf16[64,32,1,1,1]{0,4,3,2,1:T(2,128)(2,1)} %copy.271) | copy-start | bytes 12292
  292.2 49.2 %copy-start.20 = (bf16[64,32,1,8,1]{0,4,3,2,1:T(2,128)(2,1)S(1)}, bf16[64,32,1,8,1]{0,4,3,2,1:T(2,128)(2,1)}, u32[]{:S(2)}) copy-start(bf16[64,32,1,8,1]{0,4,3,2,1:T(2,128)(2,1)} %copy.264) | copy-start | bytes 98308
  292.2 61.4 %copy-start.19 = (bf16[64,32,1,8,1]{0,4,3,2,1:T(2,128)(2,1)S(1)}, bf16[64,32,1,8,1]{0,4,3,2,1:T(2,128)(2,1)}, u32[]{:S(2)}) copy-start(bf16[64,32,1,8,1]{0,4,3,2,1:T(2,128)(2,1)} %copy.269) | copy-start | bytes 98308
  362.8 21.9 %copy-start.4 = (bf16[64,32,512]{0,2,1:T(8,128)(2,1)S(1)}, bf16[64,32,512]{0,2,1:T(8,128)(2,1)}, u32[]{:S(2)}) copy-start(bf16[64,32,512]{0,2,1:T(8,128)(2,1)} %copy.210) | copy-start | bytes 6291460
  362.8 21.9 %copy-start.13 = (bf16[64,512]{0,1:T(8,128)(2,1)S(1)}, bf16[64,512]{0,1:T(8,128)(2,1)}, u32[]{:S(2)}) copy-start(bf16[64,512]{0,1:T(8,128)(2,1)} %copy-done.12) | copy-start | bytes 196612
  362.8 21.9 %copy-start.14 = (f32[64,512]{0,1:T(8,128)S(1)}, f32[64,512]{0,1:T(8,128)}, u32[]{:S(2)}) copy-start(f32[64,512]{0,1:T(8,128)} %copy.211) | copy-start | bytes 393220
  362.8 22.0 %copy-start.61 = (f32[32]{0:T(128)S(1)}, f32[32]{0:T(128)}, u32[]{:S(2)}) copy-start(f32[32]{0:T(128)} %param.83) | copy-start | bytes 388
  395.2 16.2 %copy-start.32 = (s32[16384]{0:T(1024)S(1)}, s32[16384]{0:T(1024)}, u32[]{:S(2)}) copy-start(s32[16384]{0:T(1024)} %get-tuple-element.438) | copy-start | bytes 196612
  795.1 59.9 %copy-start.25 = (s32[16384]{0:T(1024)S(1)}, s32[16384]{0:T(1024)}, u32[]{:S(2)}) copy-start(s32[16384]{0:T(1024)} %get-tuple-element.431) | copy-start | bytes 196612
  933.1 13.9 %copy-start.2 = (s32[8192,1]{0,1:T(1,128)S(1)}, s32[8192,1]{0,1:T(1,128)}, u32[]{:S(2)}) copy-start(s32[8192,1]{0,1:T(1,128)} %get-tuple-element.439) | copy-start | bytes 98308
  933.8 13.1 %all-to-all-start.2 = ((f32[32,1,512]{2,1,0:T(1,128)}), f32[32,1,512]{2,1,0:T(1,128)S(1)}, u32[]{:S(2)}, u32[]{:S(2)}) async-start(f32[32,1,512]{2,1,0:T(1,128)} %copy.293), calls=%async_computation.2 | async-start | bytes 131072 | tf_op jit(solution)/shard_map/all_to_all | solution.py:167
  946.9 100.1 %copy-start.1 = (bf16[32,32,3,3,3]{1,0,4,3,2:T(8,128)(2,1)S(1)}, bf16[32,32,3,3,3]{1,0,4,3,2:T(8,128)(2,1)}, u32[]{:S(2)}) copy-start(bf16[32,32,3,3,3]{1,0,4,3,2:T(8,128)(2,1)} %param.82) | copy-start | bytes 165892
  (40 other events, 248.1 us)
where the time goes:
time: 1060 us; the launch traced here: 1050 us
  local copies, waits for them, and re-layouts  949 us (90%)
  other arithmetic  38.1 us (4%)
  matrix products  29 us (3%)
  starting transfers between devices  27.3 us (3%)
    gather x16, local copies, waits for them, and re-layouts, trilinear_rows(): jnp.take(row_table, column, axis=0).astype(jnp.float32)  513 us
    scatter x26, local copies, waits for them, and re-layouts, per_device(): padded = padded.at[:, :, tx[0]:tx[1], ty[0]:ty[1], tz[0]:tz[1]].set(slab)  140 us
    gather x1, local copies, waits for them, and re-layouts, per_device(): point_value = returned[owner_dev, slot_index]  100 us
    unnamed x143, local copies, waits for them, and re-layouts  75 us
    gather x52, local copies, waits for them, and re-layouts, take_slab(): taken = jnp.take(slab, safe_rows, axis=0)  37.6 us
    another operation x25, local copies, waits for them, and re-layouts, take_slab(): taken = jnp.take(slab, safe_rows, axis=0)  25 us
    conv_general_dilated x1, matrix products, per_device(): lax.conv_general_dilated(padded, conv_weight, (1, 1, 1), 'VALID', dimensi...  21.9 us
  transfers between devices with their start and end apart: 5, of which 1 were waited for; matrix products, arithmetic and copies ran while one was open for 85% of the time, Pallas kernels for 0%

commit v1 on v0

v1 whole, which is shorter than its diff:
```python
import functools

import jax
import jax.numpy as jnp
from jax import lax
from jax.experimental import pallas as pl
from jax.experimental.pallas import tpu as pltpu
from jax.sharding import PartitionSpec as P

F32 = jnp.float32
BF16 = jnp.bfloat16
VMEM_BYTES = 56 * 1024 * 1024


def from_behind(value, axis, steps):
    count = lax.axis_size(axis)
    initial, last = (max(0, -steps), min(count, count - steps))
    return lax.ppermute(value, axis, [(source, source + steps) for source in range(initial, last)])


def iota(shape, axis):
    return lax.broadcasted_iota(jnp.int32, shape, axis)


def shifted(own, below, above, step, stride, coord):
    lanes = own.shape[1]
    if step == 0:
        return own
    if step > 0:
        return jnp.where(
            coord < 7, pltpu.roll(own, lanes - stride, 1), pltpu.roll(above, 7 * stride, 1)
        )
    return jnp.where(
        coord > 0, pltpu.roll(own, stride, 1), pltpu.roll(below, lanes - 7 * stride, 1)
    )


def conv_kernel(per_step, nb_ref, own_ref, prev_ref, next_ref, occ_ref, w_ref, bias_ref, out_ref, x_ref):
    lane = iota((32, 128), 1)
    z = lane & 7
    y = (lane >> 3) & 7
    low_half = lane < 64
    step_id = pl.program_id(0)
    together = x_ref.shape[0]

    def one_brick(i, k):
        b = step_id * per_step + i
        for col in range(5):
            pieces = []
            for slot in range(9):
                if col < 4:
                    piece = own_ref[nb_ref[b * 27 + 9 + slot], :, col * 128 : (col + 1) * 128]
                else:
                    piece = jnp.where(
                        low_half,
                        next_ref[nb_ref[b * 27 + 18 + slot]],
                        prev_ref[nb_ref[b * 27 + slot]],
                    )
                pieces.append(piece)
            for tz in (-1, 0, 1):
                rows = [
                    shifted(pieces[3 * j + 1], pieces[3 * j], pieces[3 * j + 2], tz, 1, z)
                    for j in range(3)
                ]
                for ty in (-1, 0, 1):
                    moved = shifted(rows[1], rows[0], rows[2], ty, 8, y)
                    at = ((ty + 1) * 3 + tz + 1) * 32
                    x_ref[k, at : at + 32, col * 128 : (col + 1) * 128] = moved
        conv = jnp.dot(w_ref[...], x_ref[k], preferred_element_type=F32)
        behind = [
            pltpu.roll(conv[0:32, c * 128 : (c + 1) * 128], 64, 1) for c in (4, 0, 1, 2, 3)
        ]
        ahead = [
            pltpu.roll(conv[64:96, c * 128 : (c + 1) * 128], 64, 1) for c in (0, 1, 2, 3, 4)
        ]
        for col in range(4):
            lanes = slice(col * 128, (col + 1) * 128)
            total = conv[32:64, lanes]
            total = total + jnp.where(low_half, behind[col], behind[col + 1])
            total = total + jnp.where(low_half, ahead[col], ahead[col + 1])
            occupied = occ_ref[b, :, lanes].astype(F32)
            center = own_ref[b, :, lanes].astype(F32)
            out_ref[i, :, lanes] = (
                center + occupied * jnp.maximum(total + bias_ref[...], 0.0)
            ).astype(BF16)

    def some_bricks(j, carry):
        for k in range(together):
            one_brick(j * together + k, k)
        return carry

    lax.fori_loop(0, per_step // together, some_bricks, 0)


def conv_block(masked, previous, following, local_nb, occupancy, conv_weight, conv_bias):
    bricks = masked.shape[0] - 1
    weight = jnp.transpose(conv_weight, (2, 0, 3, 4, 1)).reshape(96, 288)
    per_step = 8

    def whole(*shape):
        return pl.BlockSpec(shape, lambda i, nb: (0,) * len(shape))

    return pl.pallas_call(
        functools.partial(conv_kernel, per_step),
        grid_spec=pltpu.PrefetchScalarGridSpec(
            num_scalar_prefetch=1,
            grid=(bricks // per_step,),
            in_specs=[
                whole(bricks + 1, 32, 512),
                whole(bricks + 1, 32, 128),
                whole(bricks + 1, 32, 128),
                whole(bricks, 1, 512),
                whole(96, 288),
                whole(32, 1),
            ],
            out_specs=pl.BlockSpec((per_step, 32, 512), lambda i, nb: (i, 0, 0)),
            scratch_shapes=[pltpu.VMEM((4, 288, 640), BF16)],
        ),
        out_shape=jax.ShapeDtypeStruct((bricks, 32, 512), BF16),
        compiler_params=pltpu.CompilerParams(vmem_limit_bytes=VMEM_BYTES),
        cost_estimate=pl.CostEstimate(flops=4 * 10**9, bytes_accessed=6 * 2**20, transcendentals=0),
        name="conv_block",
    )(local_nb, masked, previous, following, occupancy[:, None, :], weight, conv_bias[:, None])


def dispatch_kernel(shift, width, brick_ref, cell_ref, frac_ref, send_ref, slot_ref, acc_ref):
    devices, _, capacity = send_ref.shape
    points = brick_ref.shape[1]
    before = (iota((width, width), 0) < iota((width, width), 1)).astype(BF16)
    acc_ref[...] = jnp.zeros_like(acc_ref)

    def block(i, offset):
        at = pl.ds(pl.multiple_of(i * width, width), width)
        brick = brick_ref[:, at]
        owner = lax.shift_right_logical(brick, shift)
        hit = iota((devices, width), 0) == owner
        hits = hit.astype(F32)
        rank = jnp.dot(hits.astype(BF16), before, preferred_element_type=F32) + offset
        slot = jnp.sum(hits * rank, axis=0, keepdims=True).astype(jnp.int32)
        slot_ref[:, at] = slot
        index = (brick - lax.shift_left(owner, shift)) * 512 + cell_ref[:, at]
        words = [index] + [
            (frac_ref[a : a + 1, at] * 65535.0 + 0.5).astype(jnp.int32) for a in range(3)
        ]
        rows = []
        for word in words:
            rows.append((hits * lax.shift_right_logical(word, 8).astype(F32)).astype(BF16))
            rows.append((hits * (word & 255).astype(F32)).astype(BF16))
        spread = (iota((capacity, width), 0) == slot).astype(F32).astype(BF16)
        acc_ref[...] += lax.dot_general(
            jnp.concatenate(rows, axis=0),
            spread,
            (((1,), (1,)), ((), ())),
            preferred_element_type=F32,
        )
        return offset + jnp.sum(hits, axis=1, keepdims=True)

    lax.fori_loop(0, points // width, block, jnp.zeros((devices, 1), F32))
    for word in range(4):
        high = acc_ref[2 * word * devices : (2 * word + 1) * devices, :]
        low = acc_ref[(2 * word + 1) * devices : (2 * word + 2) * devices, :]
        send_ref[:, word, :] = high * 256.0 + low


def dispatch(point_brick, point_cell, point_frac, devices, capacity, bricks):
    points = point_brick.shape[0]
    shift = bricks.bit_length() - 1
    assert bricks == 1 << shift
    return pl.pallas_call(
        functools.partial(dispatch_kernel, shift, 512),
        out_shape=(
            jax.ShapeDtypeStruct((devices, 4, capacity), F32),
            jax.ShapeDtypeStruct((1, points), jnp.int32),
        ),
        scratch_shapes=[pltpu.VMEM((8 * devices, capacity), F32)],
        compiler_params=pltpu.CompilerParams(vmem_limit_bytes=VMEM_BYTES),
        name="dispatch",
    )(point_brick[None, :], point_cell[None, :], point_frac)


def sample_kernel(blocks_ref, recv_ref, din_ref, bias_ref, dout_ref, out_ref, table_ref):
    sources, _, capacity = recv_ref.shape
    depth = table_ref.shape[1]
    bricks = depth // 8

    def turn(c, carry):
        for j in range(4):
            part = blocks_ref[c, :, j * 128 : (j + 1) * 128].astype(F32)
            both = jnp.concatenate([part, pltpu.roll(part, 64, 1)], axis=0)
            table_ref[pl.ds(pl.multiple_of(c * 64, 64), 64), j * 2 * bricks : (j + 1) * 2 * bricks] = (
                both.T[:64].astype(BF16)
            )
        return carry

    lax.fori_loop(0, 32, turn, 0)

    def chunk(s, carry):
        index = recv_ref[s, 0:1, :].astype(jnp.int32)
        fx, fy, fz = (recv_ref[s, a : a + 1, :] * (1.0 / 65535.0) for a in (1, 2, 3))
        x0 = lax.shift_right_logical(index, 6) & 7
        xb = x0 * bricks + lax.shift_right_logical(index, 9)
        row = iota((depth, capacity), 0)
        along_x = jnp.where(
            row == xb, 1.0 - fx, jnp.where(row == xb + bricks, fx, 0.0)
        ).astype(BF16)
        yz = iota((64, capacity), 0)
        y0 = lax.shift_right_logical(index, 3) & 7
        z0 = index & 7
        ry, rz = lax.shift_right_logical(yz, 3), yz & 7
        along_y = jnp.where(ry == y0, 1.0 - fy, jnp.where(ry == y0 + 1, fy, 0.0))
        along_z = jnp.where(rz == z0, 1.0 - fz, jnp.where(rz == z0 + 1, fz, 0.0))
        weight = along_y * along_z
        sums = []
        for part in range(4):
            found = jnp.dot(
                table_ref[part * 512 : (part + 1) * 512, :], along_x, preferred_element_type=F32
            )
            for c in range(8):
                rows = [
                    found[c * 64 + k : c * 64 + k + 8, :] * weight[k : k + 8, :]
                    for k in range(0, 64, 8)
                ]
                while len(rows) > 1:
                    rows = [p + q for p, q in zip(rows[::2], rows[1::2])]
                sums.append(rows[0])
        sample = jnp.concatenate(sums, axis=0).astype(BF16)
        hidden = jnp.maximum(
            jnp.dot(din_ref[...], sample, preferred_element_type=F32) + bias_ref[...],
            0.0,
        ).astype(BF16)
        out_ref[s] = jnp.sum(hidden.astype(F32) * dout_ref[...], axis=0, keepdims=True)
        return carry

    lax.fori_loop(0, sources, chunk, 0)


def sample_points(block_out, received, decoder_in, decoder_bias, decoder_out):
    bricks = block_out.shape[0]
    sources, _, capacity = received.shape
    return pl.pallas_call(
        sample_kernel,
        out_shape=jax.ShapeDtypeStruct((sources, 1, capacity), F32),
        scratch_shapes=[pltpu.VMEM((2048, bricks * 8), BF16)],
        compiler_params=pltpu.CompilerParams(vmem_limit_bytes=VMEM_BYTES),
        name="sample_points",
    )(
        jnp.transpose(block_out, (1, 0, 2)),
        received,
        jnp.repeat(decoder_in, 8, axis=1),
        decoder_bias[:, None],
        decoder_out.astype(F32)[:, None],
    )[:, 0, :]


def collect_kernel(shift, width, brick_ref, slot_ref, back_ref, out_ref):
    devices, capacity = back_ref.shape
    points = brick_ref.shape[1]
    back = back_ref[...]
    high = back.astype(BF16)
    rest = back - high.astype(F32)
    mid = rest.astype(BF16)
    low = (rest - mid.astype(F32)).astype(BF16)
    pieces = jnp.concatenate([high, mid, low], axis=0)

    def block(i, carry):
        at = pl.ds(pl.multiple_of(i * width, width), width)
        owner = lax.shift_right_logical(brick_ref[:, at], shift)
        spread = (iota((capacity, width), 0) == slot_ref[:, at]).astype(F32).astype(BF16)
        found = jnp.dot(pieces, spread, preferred_element_type=F32)
        value = found[:devices] + found[devices : 2 * devices] + found[2 * devices :]
        hit = iota((devices, width), 0) == owner
        out_ref[:, at] = jnp.sum(jnp.where(hit, value, 0.0), axis=0, keepdims=True)
        return carry

    lax.fori_loop(0, points // width, block, 0)


def collect(point_brick, slot, back, bricks):
    points = point_brick.shape[0]
    return pl.pallas_call(
        functools.partial(collect_kernel, bricks.bit_length() - 1, 512),
        out_shape=jax.ShapeDtypeStruct((1, points), F32),
        compiler_params=pltpu.CompilerParams(vmem_limit_bytes=VMEM_BYTES),
        name="collect",
    )(point_brick[None, :], slot, back)[0]


def per_device(
    features,
    occupancy,
    neighbours,
    conv_weight,
    conv_bias,
    point_brick,
    point_cell,
    point_frac,
    decoder_in,
    decoder_bias,
    decoder_out,
):
    axes = ("grp", "dev")
    bricks = features.shape[0]
    devices = lax.axis_size(axes)
    me = lax.axis_index(axes)
    capacity = 2 * point_brick.shape[0] // devices
    send, slot = dispatch(point_brick, point_cell, point_frac, devices, capacity, bricks)
    received = lax.all_to_all(send, axes, split_axis=0, concat_axis=0, tiled=True)
    masked = features * occupancy[:, None, :].astype(features.dtype)
    masked = jnp.pad(masked, ((0, 1), (0, 0), (0, 0)))
    previous = from_behind(masked[:, :, 384:], axes, 1)
    following = from_behind(masked[:, :, :128], axes, -1)
    first = (me + jnp.repeat(jnp.arange(-1, 2, dtype=jnp.int32), 9)) * bricks
    local_nb = jnp.where(
        neighbours >= 0, jnp.clip(neighbours - first[None, :], 0, bricks - 1), bricks
    ).reshape(-1)
    block_out = conv_block(
        masked, previous, following, local_nb, occupancy, conv_weight, conv_bias
    )
    values = sample_points(block_out, received, decoder_in, decoder_bias, decoder_out)
    back = lax.all_to_all(values, axes, split_axis=0, concat_axis=0, tiled=True)
    return block_out, collect(point_brick, slot, back, bricks)


def solution(mesh):
    axes = ("grp", "dev")
    return jax.shard_map(
        per_device,
        mesh=mesh,
        in_specs=(
            P(axes, None, None),
            P(axes, None),
            P(axes, None),
            P(),
            P(),
            P(axes),
            P(axes),
            P(None, axes),
            P(),
            P(),
            P(),
        ),
        out_specs=(P(axes, None, None), P(axes)),
        check_vma=False,
    )
```

time: 1060 us -> 184 us (0.17); the launches traced: 1050 us -> 183 us
  local copies, waits for them, and re-layouts: 949 us -> 13.5 us
  Pallas kernels: 0 us -> 140 us
  other arithmetic: 38.1 us -> 2.77 us
  matrix products: 29 us -> 0 us
  starting transfers between devices: 27.3 us -> 12.9 us
  blocking collectives: 0 us -> 13.2 us
    gather x69 -> x0, local copies, waits for them, and re-layouts: 650 us -> none  [the longest x16 513 us: trilinear_rows(): jnp.take(row_table, column, axis=0).astype(jnp.float32)]
    pallas_call x0 -> x4, Pallas kernels: none -> 140 us  [the longest x1 65.3 us: conv_block(): pl.pallas_call(functools.partial(conv_kernel, per_step), grid_spec=pltpu....]
    scatter x26 -> x0, local copies, waits for them, and re-layouts: 140 us -> none  [per_device(): padded = padded.at[:, :, tx[0]:tx[1], ty[0]:ty[1], tz[0]:tz[1]].set(slab)]
    unnamed x143 -> x15, local copies, waits for them, and re-layouts: 75 us -> 1.35 us
    another operation x26 -> x0, local copies, waits for them, and re-layouts: 27.7 us -> none  [the longest x25 25 us: take_slab(): taken = jnp.take(slab, safe_rows, axis=0)]
    conv_general_dilated x1 -> x0, matrix products: 21.9 us -> none  [per_device(): lax.conv_general_dilated(padded, conv_weight, (1, 1, 1), 'VALID', dimensi...]
    transpose x2 -> x1, local copies, waits for them, and re-layouts: 19 us -> 0.15 us  [conv_block(): weight = jnp.transpose(conv_weight, (2, 0, 3, 4, 1)).reshape(96, 288)]
    all_to_all x3 -> x1, starting transfers between devices: 22.2 us -> 8.41 us  [per_device(): lax.all_to_all(send, axes, split_axis=0, concat_axis=0, tiled=True)]
  transfers between devices with their start and end apart: 5 -> 3, of which waited for: 1 -> 0; matrix products, arithmetic and copies ran while one was open for 85% -> 7% of each run, Pallas kernels for 0% -> 41%
where the time goes in v1:
time: 184 us; the launch traced here: 183 us
  Pallas kernels  140 us (76%)
  local copies, waits for them, and re-layouts  13.5 us (7%)
  blocking collectives  13.2 us (7%)
  starting transfers between devices  12.9 us (7%)
  other arithmetic  2.77 us (2%)
    pallas_call x1, Pallas kernels, conv_block(): pl.pallas_call(functools.partial(conv_kernel, per_step), grid_spec=pltpu....  65.3 us
    pallas_call x1, Pallas kernels, sample_points(): pl.pallas_call(sample_kernel, out_shape=jax.ShapeDtypeStruct((sources, 1,...  58.9 us
    all_to_all x1, blocking collectives, per_device(): back = lax.all_to_all(values, axes, split_axis=0, concat_axis=0, tiled=True)  13.2 us
    pallas_call x1, Pallas kernels, dispatch(): pl.pallas_call(functools.partial(dispatch_kernel, shift, 512), out_shape=...  10.5 us
    all_to_all x1, starting transfers between devices, per_device(): lax.all_to_all(send, axes, split_axis=0, concat_axis=0, tiled=True)  8.41 us
    pallas_call x1, Pallas kernels, collect(): pl.pallas_call(functools.partial(collect_kernel, bricks.bit_length() - 1,...  5.35 us
    ppermute x2, starting transfers between devices, from_behind(): lax.ppermute(value, axis, [(source, source + steps) for source in range(i...  4.46 us
    pallas_call x1, local copies, waits for them, and re-layouts, conv_block(): pl.pallas_call(functools.partial(conv_kernel, per_step), grid_spec=pltpu....  4.08 us
  transfers between devices with their start and end apart: 3, of which 0 were waited for; matrix products, arithmetic and copies ran while one was open for 7% of the time, Pallas kernels for 41%

profile of v1, /device:TPU:0, one launch (start us, length us, event | category | flops | bytes accessed | tf_op | source)
XLA Modules:
  0.0 183.1 jit_solution(15854519152591280103)
XLA Ops:
  0.6 0.0 copy-start
  0.6 0.9 convert_element_type.7
  1.6 1.8 broadcast_multiply_fusion
  3.3 0.0 copy-start.3
  3.3 0.2 pad_slice_fusion
  3.5 3.2 %collective-permute-start = (bf16[65,32,128]{2,1,0:T(8,128)(2,1)S(1)}, bf16[65,32,128]{2,1,0:T(8,128)(2,1)}, u32[]{:S(2)}, u32[]{:S(2)}) collective-permute-start(bf16[65,32,128]{2,1,0:T(8,128)(2,1)S(1)} %get-tuple-element.7), channel_id=1, source_target_pairs={{0,1},{1,2},{2,3},{3,4},{4,5},{5,6},{6,7},{7,8},{8,9},{9,10},{10,1... | collective-permute-start | bytes 1597448 | tf_op jit(solution)/shard_map/ppermute | solution.py:18
  6.7 1.3 collective-permute-start.1
  8.0 10.5 %dispatch.1 = (f32[32,4,512]{2,1,0:T(4,128)}, s32[1,8192]{1,0:T(1,128)}) custom-call(s32[1,8192]{1,0:T(1,128)} %bitcast.20, s32[1,8192]{1,0:T(1,128)} %bitcast.23, f32[3,8192]{1,0:T(4,128)} %frac_ref.1), custom_call_target="tpu_custom_call" | custom-call | tf_op jit(solution)/shard_map/dispatch/pallas_call | solution.py:169
  18.5 8.4 %all-to-all-start = ((f32[32,4,512]{2,1,0:T(4,128)}), f32[32,4,512]{2,1,0:T(4,128)S(1)}, u32[]{:S(2)}, u32[]{:S(2)}) async-start(f32[32,4,512]{2,1,0:T(4,128)} %get-tuple-element.5), calls=%async_computation | async-start | bytes 524288 | tf_op jit(solution)/shard_map/all_to_all | solution.py:307
  26.9 0.1 broadcast_in_dim.33
  27.0 0.1 mul.24
  27.1 0.1 clamp_select_fusion
  27.2 1.7 broadcast_in_dim.35.occ_ref
  28.8 0.1 copy.28
  28.9 0.7 reshape.29.nb_ref
  29.6 1.5 pad.4.own_ref
  31.1 0.2 copy.29
  31.3 0.8 reshape.30.w_ref
  32.1 0.7 copy.30.bias_ref
  32.8 0.7 copy.32.din_ref
  33.5 0.7 copy.34.dout_ref
  34.2 0.7 copy.33.bias_ref
  34.9 0.0 collective-permute-done.prev_ref
  34.9 0.0 collective-permute-done.1.next_ref
  34.9 65.3 %conv_block.1 = bf16[64,32,512]{2,1,0:T(8,128)(2,1)} custom-call(s32[1728]{0:T(1024)} %reshape.29.nb_ref, bf16[65,32,512]{2,1,0:T(8,128)(2,1)} %pad.4.own_ref, bf16[65,32,128]{2,1,0:T(8,128)(2,1)} %collective-permute-done.prev_ref, bf16[65,32,128]{2,1,0:T(8,128)(2,1)} %collective-permute-done.1.next_ref, s32[64,1,512]{2,1,0:T(1,128)} %broadcast_in_dim.35.occ_ref, ...), custom_call_target="tpu_custom_call" | custom-call | flops 4000000000 | bytes 6291456 | tf_op jit(solution)/shard_map/conv_block/pallas_call | solution.py:103
  100.2 4.1 %copy.38 = bf16[64,32,512]{2,0,1:T(8,128)(2,1)} copy(bf16[64,32,512]{2,1,0:T(8,128)(2,1)} %conv_block.1) | data formatting | bytes 4194304 | tf_op jit(solution)/shard_map/conv_block/pallas_call | solution.py:103
  104.3 0.0 all-to-all-done.recv_ref
  104.3 0.7 copy-done.1
  105.0 58.9 %sample_points.1 = f32[32,1,512]{2,1,0:T(1,128)} custom-call(bf16[32,64,512]{2,1,0:T(8,128)(2,1)} %bitcast.17, f32[32,4,512]{2,1,0:T(4,128)} %copy-done.1, bf16[64,256]{1,0:T(8,128)(2,1)} %copy.32.din_ref, f32[64,1]{1,0:T(8,128)} %copy.33.bias_ref, f32[64,1]{1,0:T(8,128)} %copy.34.dout_ref), custom_call_target="tpu_custom_call" | custom-call | tf_op jit(solution)/shard_map/sample_points/pallas_call | solution.py:240
  163.9 13.2 %all_to_all.13 = f32[32,1,512]{2,1,0:T(1,128)S(1)} all-to-all(f32[32,1,512]{2,1,0:T(1,128)} %sample_points.1), channel_id=1, replica_groups=mesh['grp'=4,'dev'=8] {'grp','dev'}, dimensions={0} | all-to-all | bytes 131072 | tf_op jit(solution)/shard_map/all_to_all | solution.py:320
  177.1 0.6 copy.39
  177.8 5.4 %collect.1 = f32[1,8192]{1,0:T(1,128)} custom-call(s32[1,8192]{1,0:T(1,128)} %bitcast.21, s32[1,8192]{1,0:T(1,128)} %get-tuple-element.4.slot_ref, f32[32,512]{1,0:T(8,128)} %bitcast.18), custom_call_target="tpu_custom_call" | custom-call | tf_op jit(solution)/shard_map/collect/pallas_call | solution.py:280
  (14 shorter events, 0.0 us)
Async XLA Ops:
  0.6 32.2 %copy-start = (bf16[64,32]{0,1:T(8,128)(2,1)S(1)}, bf16[64,32]{0,1:T(8,128)(2,1)}, u32[]{:S(2)}) copy-start(bf16[64,32]{0,1:T(8,128)(2,1)} %param.19) | copy-start | bytes 12292
  3.3 23.7 %copy-start.3 = (s32[64,27]{0,1:T(8,128)S(1)}, s32[64,27]{0,1:T(8,128)}, u32[]{:S(2)}) copy-start(s32[64,27]{0,1:T(8,128)} %param.13) | copy-start | bytes 20740
  3.5 31.4 %collective-permute-start = (bf16[65,32,128]{2,1,0:T(8,128)(2,1)S(1)}, bf16[65,32,128]{2,1,0:T(8,128)(2,1)}, u32[]{:S(2)}, u32[]{:S(2)}) collective-permute-start(bf16[65,32,128]{2,1,0:T(8,128)(2,1)S(1)} %get-tuple-element.7), channel_id=1, source_target_pairs={{0,1},{1,2},{2,3},{3,4},{4,5},{5,6},{6,7},{7,8},{8,9},{9,10},{10,1... | collective-permute-start | bytes 1597448 | tf_op jit(solution)/shard_map/ppermute | solution.py:18
  6.7 28.2 %collective-permute-start.1 = (bf16[65,32,128]{2,1,0:T(8,128)(2,1)S(1)}, bf16[65,32,128]{2,1,0:T(8,128)(2,1)}, u32[]{:S(2)}, u32[]{:S(2)}) collective-permute-start(bf16[65,32,128]{2,1,0:T(8,128)(2,1)S(1)} %get-tuple-element.6), channel_id=1, source_target_pairs={{1,0},{2,1},{3,2},{4,3},{5,4},{6,5},{7,6},{8,7},{9,8},{10,9},{11,1... | collective-permute-start | bytes 1597448 | tf_op jit(solution)/shard_map/ppermute | solution.py:18
  18.5 85.8 %all-to-all-start = ((f32[32,4,512]{2,1,0:T(4,128)}), f32[32,4,512]{2,1,0:T(4,128)S(1)}, u32[]{:S(2)}, u32[]{:S(2)}) async-start(f32[32,4,512]{2,1,0:T(4,128)} %get-tuple-element.5), calls=%async_computation | async-start | bytes 524288 | tf_op jit(solution)/shard_map/all_to_all | solution.py:307
  29.6 1.5 copy-start.2
  29.6 2.5 %copy-start.5 = (f32[32]{0:T(128)S(1)}, f32[32]{0:T(128)}, u32[]{:S(2)}) copy-start(f32[32]{0:T(128)} %param.15) | copy-start | bytes 388
  29.6 3.9 %copy-start.6 = (bf16[64]{0:T(256)(128)(2,1)S(1)}, bf16[64]{0:T(256)(128)(2,1)}, u32[]{:S(2)}) copy-start(bf16[64]{0:T(256)(128)(2,1)} %param.21) | copy-start | bytes 388
  29.6 4.6 %copy-start.4 = (f32[64]{0:T(128)S(1)}, f32[64]{0:T(128)}, u32[]{:S(2)}) copy-start(f32[64]{0:T(128)} %param.20) | copy-start | bytes 772
  104.3 0.7 copy-start.1

commit v2 on v1

v2 whole, which is shorter than its diff:
```python
import functools

import jax
import jax.numpy as jnp
from jax import lax
from jax.experimental import pallas as pl
from jax.experimental.pallas import tpu as pltpu
from jax.sharding import PartitionSpec as P

F32 = jnp.float32
BF16 = jnp.bfloat16
VMEM_BYTES = 56 * 1024 * 1024


def from_behind(value, axis, steps):
    count = lax.axis_size(axis)
    initial, last = (max(0, -steps), min(count, count - steps))
    return lax.ppermute(value, axis, [(source, source + steps) for source in range(initial, last)])


def iota(shape, axis):
    return lax.broadcasted_iota(jnp.int32, shape, axis)


def conv_kernel(per_step, nb_ref, own_ref, prev_ref, next_ref, occ_ref, w_ref, bias_ref, out_ref, x_ref, edge_ref, prev_edge_ref, next_edge_ref):
    lane = iota((8, 128), 1)
    row = iota((8, 128), 0)
    bricks = own_ref.shape[0]

    def edges(lanes):
        both = jnp.where(
            iota(lanes.shape[:-1] + (128,), len(lanes.shape) - 1) < 32,
            pltpu.roll(lanes[..., 128:], 32, len(lanes.shape) - 1),
            pltpu.roll(lanes[..., :128], 32, len(lanes.shape) - 1),
        )
        again = pltpu.roll(both, 64, len(lanes.shape) - 1)
        return jnp.where(iota(both.shape, len(lanes.shape) - 1) < 64, both, again)

    @pl.when(pl.program_id(0) == 0)
    def _():
        def fill(b, carry):
            for x in range(8):
                edge_ref[b, x] = edges(own_ref[b, x])
            prev_edge_ref[b] = edges(prev_ref[b])
            next_edge_ref[b] = edges(next_ref[b])
            return carry

        lax.fori_loop(0, bricks, fill, 0)

    def moved(below, here, above):
        back = pltpu.roll(jnp.where(row == 7, below, here), 1, 0)
        forth = pltpu.roll(jnp.where(row == 0, above, here), 7, 0)
        return back, here, forth

    first = pl.program_id(0) * per_step

    def one_brick(i, carry):
        base = (first + i) * 27
        columns = []
        for x in range(-1, 9):
            group = 0 if x < 0 else (2 if x > 7 else 1)
            names = [nb_ref[base + group * 9 + slot] for slot in range(9)]
            if group == 0:
                whole, edge = (lambda n: prev_ref[n]), (lambda n: prev_edge_ref[n])
            elif group == 2:
                whole, edge = (lambda n: next_ref[n]), (lambda n: next_edge_ref[n])
            else:
                whole, edge = (lambda n: own_ref[n, x]), (lambda n: edge_ref[n, x])
            lines = [whole(names[3 * j + 1]) for j in range(3)]
            low = moved(*[line[:, :128] for line in lines])
            high = moved(*[line[:, 128:] for line in lines])
            ends = moved(
                *[
                    jnp.where((lane & 63) < 32, edge(names[3 * j]), edge(names[3 * j + 2]))
                    for j in range(3)
                ]
            )
            columns.append(
                [low[0], high[0], low[1], high[1], low[2], high[2]]
                + [jnp.where(lane < 64, ends[0], ends[2]), ends[1]]
            )
        for pair in range(5):
            at = pl.ds(pl.multiple_of(i * 80 + pair * 16, 16), 16)
            for k in range(8):
                x_ref[at, k * 128 : (k + 1) * 128] = jnp.concatenate(
                    [columns[2 * pair][k], columns[2 * pair + 1][k]], axis=0
                ).astype(BF16)
        return carry

    lax.fori_loop(0, per_step, one_brick, 0)
    found = jnp.dot(x_ref[...], w_ref[...], preferred_element_type=F32)
    for i in range(per_step):
        total = bias_ref[...]
        for tx in range(3):
            at = i * 80 + tx * 8
            total = total + found[at : at + 64, tx * 256 : (tx + 1) * 256]
        center = own_ref[first + i].reshape(64, 256)
        occupied = occ_ref[i].reshape(64, 256).astype(F32)
        out_ref[i] = (center + occupied * jnp.maximum(total, 0.0)).reshape(8, 8, 256)


def banded_weight(conv_weight):
    taps = jnp.transpose(conv_weight, (3, 1, 2, 4, 0))[:, :, :, ::-1, :].reshape(3, 32, 3, 96)
    wide = jnp.pad(taps, ((0, 0), (0, 0), (0, 0), (256, 256)))
    rows = []
    for z in range(-1, 9):
        start = 256 - (z - 1) * 32
        rows.append(wide[:, :, :, start : start + 256].reshape(3, 32, 768))
    own = jnp.stack(rows[1:9], axis=1).reshape(768, 768)
    ends = jnp.concatenate([rows[0], rows[9]], axis=1)
    return jnp.concatenate([own, ends[0], ends[2], ends[1], jnp.zeros_like(ends[1])], axis=0)


def conv_block(masked, previous, following, local_nb, occupancy, conv_weight, conv_bias):
    bricks = masked.shape[0] - 1
    weight = banded_weight(conv_weight)
    per_step = 8

    def whole(*shape):
        return pl.BlockSpec(shape, lambda i, nb: (0,) * len(shape))

    def part(*shape):
        return pl.BlockSpec((per_step,) + shape, lambda i, nb: (i,) + (0,) * len(shape))

    occupied = jnp.repeat(occupancy.reshape(bricks, 64, 8).astype(BF16), 32, axis=2)
    return pl.pallas_call(
        functools.partial(conv_kernel, per_step),
        grid_spec=pltpu.PrefetchScalarGridSpec(
            num_scalar_prefetch=1,
            grid=(bricks // per_step,),
            in_specs=[
                whole(bricks + 1, 8, 8, 256),
                whole(bricks + 1, 8, 256),
                whole(bricks + 1, 8, 256),
                part(64, 256),
                whole(1024, 768),
                whole(1, 256),
            ],
            out_specs=part(8, 8, 256),
            scratch_shapes=[
                pltpu.VMEM((per_step * 80, 1024), BF16),
                pltpu.VMEM((bricks + 1, 8, 8, 128), F32),
                pltpu.VMEM((bricks + 1, 8, 128), F32),
                pltpu.VMEM((bricks + 1, 8, 128), F32),
            ],
        ),
        out_shape=jax.ShapeDtypeStruct((bricks, 8, 8, 256), F32),
        compiler_params=pltpu.CompilerParams(vmem_limit_bytes=VMEM_BYTES),
        cost_estimate=pl.CostEstimate(flops=8 * 10**9, bytes_accessed=12 * 2**20, transcendentals=0),
        name="conv_block",
    )(local_nb, masked, previous, following, occupied, weight, jnp.tile(conv_bias, 8)[None, :])


def dispatch_kernel(shift, width, brick_ref, cell_ref, frac_ref, send_ref, slot_ref, acc_ref):
    devices, _, capacity = send_ref.shape
    points = brick_ref.shape[1]
    before = (iota((width, width), 0) < iota((width, width), 1)).astype(BF16)
    acc_ref[...] = jnp.zeros_like(acc_ref)

    def block(i, offset):
        at = pl.ds(pl.multiple_of(i * width, width), width)
        brick = brick_ref[:, at]
        owner = lax.shift_right_logical(brick, shift)
        hit = iota((devices, width), 0) == owner
        hits = hit.astype(F32)
        rank = jnp.dot(hits.astype(BF16), before, preferred_element_type=F32) + offset
        slot = jnp.sum(hits * rank, axis=0, keepdims=True).astype(jnp.int32)
        slot_ref[:, at] = slot
        index = (brick - lax.shift_left(owner, shift)) * 512 + cell_ref[:, at]
        words = [index] + [
            (frac_ref[a : a + 1, at] * 65535.0 + 0.5).astype(jnp.int32) for a in range(3)
        ]
        rows = []
        for word in words:
            rows.append((hits * lax.shift_right_logical(word, 8).astype(F32)).astype(BF16))
            rows.append((hits * (word & 255).astype(F32)).astype(BF16))
        spread = (iota((capacity, width), 0) == slot).astype(F32).astype(BF16)
        acc_ref[...] += lax.dot_general(
            jnp.concatenate(rows, axis=0),
            spread,
            (((1,), (1,)), ((), ())),
            preferred_element_type=F32,
        )
        return offset + jnp.sum(hits, axis=1, keepdims=True)

    lax.fori_loop(0, points // width, block, jnp.zeros((devices, 1), F32))
    for word in range(4):
        high = acc_ref[2 * word * devices : (2 * word + 1) * devices, :]
        low = acc_ref[(2 * word + 1) * devices : (2 * word + 2) * devices, :]
        send_ref[:, word, :] = high * 256.0 + low


def dispatch(point_brick, point_cell, point_frac, devices, capacity, bricks):
    points = point_brick.shape[0]
    shift = bricks.bit_length() - 1
    assert bricks == 1 << shift
    return pl.pallas_call(
        functools.partial(dispatch_kernel, shift, 512),
        out_shape=(
            jax.ShapeDtypeStruct((devices, 4, capacity), F32),
            jax.ShapeDtypeStruct((1, points), jnp.int32),
        ),
        scratch_shapes=[pltpu.VMEM((8 * devices, capacity), F32)],
        compiler_params=pltpu.CompilerParams(vmem_limit_bytes=VMEM_BYTES),
        name="dispatch",
    )(point_brick[None, :], point_cell[None, :], point_frac)


def sample_kernel(blocks_ref, recv_ref, din_ref, bias_ref, dout_ref, out_ref, table_ref):
    sources, _, capacity = recv_ref.shape
    depth = table_ref.shape[1]
    for x in range(8):
        table_ref[x * 256 : (x + 1) * 256, :] = blocks_ref[:, x].reshape(depth, 256).T.astype(BF16)

    def chunk(s, carry):
        index = recv_ref[s, 0:1, :].astype(jnp.int32)
        fx, fy, fz = (recv_ref[s, a : a + 1, :] * (1.0 / 65535.0) for a in (1, 2, 3))
        by = lax.shift_right_logical(index, 9) * 8 + (lax.shift_right_logical(index, 3) & 7)
        row = iota((depth, capacity), 0)
        along_y = jnp.where(
            row == by, 1.0 - fy, jnp.where(row == by + 1, fy, 0.0)
        ).astype(BF16)
        xz = iota((64, capacity), 0)
        x0 = lax.shift_right_logical(index, 6) & 7
        z0 = index & 7
        rx, rz = lax.shift_right_logical(xz, 3), xz & 7
        along_x = jnp.where(rx == x0, 1.0 - fx, jnp.where(rx == x0 + 1, fx, 0.0))
        along_z = jnp.where(rz == z0, 1.0 - fz, jnp.where(rz == z0 + 1, fz, 0.0))
        weight = along_x * along_z
        sample = jnp.zeros((32, capacity), F32)
        for part in range(4):
            found = jnp.dot(
                table_ref[part * 512 : (part + 1) * 512, :], along_y, preferred_element_type=F32
            )
            for j in range(16):
                k = part * 16 + j
                sample = sample + found[j * 32 : (j + 1) * 32, :] * weight[k : k + 1, :]
        sample = sample.astype(BF16)
        hidden = jnp.maximum(
            jnp.dot(din_ref[...], sample, preferred_element_type=F32) + bias_ref[...],
            0.0,
        ).astype(BF16)
        out_ref[s] = jnp.sum(hidden.astype(F32) * dout_ref[...], axis=0, keepdims=True)
        return carry

    lax.fori_loop(0, sources, chunk, 0)


def sample_points(blocks, received, decoder_in, decoder_bias, decoder_out):
    bricks = blocks.shape[0]
    sources, _, capacity = received.shape
    return pl.pallas_call(
        sample_kernel,
        out_shape=jax.ShapeDtypeStruct((sources, 1, capacity), F32),
        scratch_shapes=[pltpu.VMEM((2048, bricks * 8), BF16)],
        compiler_params=pltpu.CompilerParams(vmem_limit_bytes=VMEM_BYTES),
        name="sample_points",
    )(
        blocks,
        received,
        decoder_in,
        decoder_bias[:, None],
        decoder_out.astype(F32)[:, None],
    )[:, 0, :]


def collect_kernel(shift, width, brick_ref, slot_ref, back_ref, out_ref):
    devices, capacity = back_ref.shape
    points = brick_ref.shape[1]
    back = back_ref[...]
    high = back.astype(BF16)
    rest = back - high.astype(F32)
    mid = rest.astype(BF16)
    low = (rest - mid.astype(F32)).astype(BF16)
    pieces = jnp.concatenate([high, mid, low], axis=0)

    def block(i, carry):
        at = pl.ds(pl.multiple_of(i * width, width), width)
        owner = lax.shift_right_logical(brick_ref[:, at], shift)
        spread = (iota((capacity, width), 0) == slot_ref[:, at]).astype(F32).astype(BF16)
        found = jnp.dot(pieces, spread, preferred_element_type=F32)
        value = found[:devices] + found[devices : 2 * devices] + found[2 * devices :]
        hit = iota((devices, width), 0) == owner
        out_ref[:, at] = jnp.sum(jnp.where(hit, value, 0.0), axis=0, keepdims=True)
        return carry

    lax.fori_loop(0, points // width, block, 0)


def collect(point_brick, slot, back, bricks):
    points = point_brick.shape[0]
    return pl.pallas_call(
        functools.partial(collect_kernel, bricks.bit_length() - 1, 512),
        out_shape=jax.ShapeDtypeStruct((1, points), F32),
        compiler_params=pltpu.CompilerParams(vmem_limit_bytes=VMEM_BYTES),
        name="collect",
    )(point_brick[None, :], slot, back)[0]


def per_device(
    features,
    occupancy,
    neighbours,
    conv_weight,
    conv_bias,
    point_brick,
    point_cell,
    point_frac,
    decoder_in,
    decoder_bias,
    decoder_out,
):
    axes = ("grp", "dev")
    bricks = features.shape[0]
    devices = lax.axis_size(axes)
    me = lax.axis_index(axes)
    capacity = 2 * point_brick.shape[0] // devices
    send, slot = dispatch(point_brick, point_cell, point_frac, devices, capacity, bricks)
    received = lax.all_to_all(send, axes, split_axis=0, concat_axis=0, tiled=True)
    masked = features * occupancy[:, None, :].astype(features.dtype)
    masked = jnp.pad(masked, ((0, 1), (0, 0), (0, 0)))
    masked = jnp.transpose(masked.reshape(bricks + 1, 32, 64, 8), (0, 2, 3, 1)).reshape(
        bricks + 1, 8, 8, 256
    )
    previous = from_behind(masked[:, 7], axes, 1).astype(F32)
    following = from_behind(masked[:, 0], axes, -1).astype(F32)
    masked = masked.astype(F32)
    first = (me + jnp.repeat(jnp.arange(-1, 2, dtype=jnp.int32), 9)) * bricks
    local_nb = jnp.where(
        neighbours >= 0, jnp.clip(neighbours - first[None, :], 0, bricks - 1), bricks
    ).reshape(-1)
    blocks = conv_block(
        masked, previous, following, local_nb, occupancy, conv_weight, conv_bias
    )
    block_out = jnp.transpose(
        blocks.astype(BF16).reshape(bricks, 64, 8, 32), (0, 3, 1, 2)
    ).reshape(bricks, 32, 512)
    values = sample_points(blocks, received, decoder_in, decoder_bias, decoder_out)
    back = lax.all_to_all(values, axes, split_axis=0, concat_axis=0, tiled=True)
    return block_out, collect(point_brick, slot, back, bricks)


def solution(mesh):
    axes = ("grp", "dev")
    return jax.shard_map(
        per_device,
        mesh=mesh,
        in_specs=(
            P(axes, None, None),
            P(axes, None),
            P(axes, None),
            P(),
            P(),
            P(axes),
            P(axes),
            P(None, axes),
            P(),
            P(),
            P(),
        ),
        out_specs=(P(axes, None, None), P(axes)),
        check_vma=False,
    )
```

time: 184 us -> 196 us (1.065)
  local copies, waits for them, and re-layouts: 13.5 us -> 69.2 us
  Pallas kernels: 140 us -> 94.7 us
  blocking collectives: 13.2 us -> 0 us
  other arithmetic: 2.77 us -> 11.9 us
  starting transfers between devices: 12.9 us -> 18.7 us
    pallas_call x1, Pallas kernels: 65.3 us -> 27.7 us  [conv_block(): pl.pallas_call(functools.partial(conv_kernel, per_step), grid_spec=pltpu....]
    unnamed x15 -> x41, local copies, waits for them, and re-layouts: 1.35 us -> 27.1 us
    another operation x0 -> x12, local copies, waits for them, and re-layouts: none -> 13.8 us  [the longest x10 13.2 us: banded_weight(): own = jnp.stack(rows[1:9], axis=1).reshape(768, 768)]
    all_to_all x1 -> x0, blocking collectives: 13.2 us -> none  [per_device(): back = lax.all_to_all(values, axes, split_axis=0, concat_axis=0, tiled=True)]
    convert_element_type x0 -> x5, other arithmetic: none -> 9.29 us  [the longest x1 2.53 us: per_device(): masked = masked.astype(F32)]
    reshape x3 -> x5, local copies, waits for them, and re-layouts: 1.54 us -> 10.6 us  [the longest x1 5.35 us: per_device(): jnp.transpose(masked.reshape(bricks + 1, 32, 64, 8), (0, 2, 3, 1))]
    pallas_call x1, Pallas kernels: 58.9 us -> 51.2 us  [sample_points(): pl.pallas_call(sample_kernel, out_shape=jax.ShapeDtypeStruct((sources, 1,...]
    transpose x1 -> x2, local copies, waits for them, and re-layouts: 0.15 us -> 6.09 us  [per_device(): jnp.transpose(masked.reshape(bricks + 1, 32, 64, 8), (0, 2, 3, 1))]
  transfers between devices with their start and end apart: 3 -> 4, of which waited for: 0 -> 0; matrix products, arithmetic and copies ran while one was open for 7% -> 32% of each run, Pallas kernels for 41% -> 20%
where the time goes in v2:
time: 196 us; the launch traced here: 195 us
  Pallas kernels  94.7 us (48%)
  local copies, waits for them, and re-layouts  69.2 us (35%)
  starting transfers between devices  18.7 us (10%)
  other arithmetic  11.9 us (6%)
    pallas_call x1, Pallas kernels, sample_points(): pl.pallas_call(sample_kernel, out_shape=jax.ShapeDtypeStruct((sources, 1,...  51.2 us
    pallas_call x1, Pallas kernels, conv_block(): pl.pallas_call(functools.partial(conv_kernel, per_step), grid_spec=pltpu....  27.7 us
    unnamed x41, local copies, waits for them, and re-layouts  27.1 us
    another operation x10, local copies, waits for them, and re-layouts, banded_weight(): own = jnp.stack(rows[1:9], axis=1).reshape(768, 768)  13.2 us
    pallas_call x1, Pallas kernels, dispatch(): pl.pallas_call(functools.partial(dispatch_kernel, shift, 512), out_shape=...  10.5 us
    all_to_all x1, starting transfers between devices, per_device(): lax.all_to_all(send, axes, split_axis=0, concat_axis=0, tiled=True)  8.82 us
    transpose x2, local copies, waits for them, and re-layouts, per_device(): jnp.transpose(masked.reshape(bricks + 1, 32, 64, 8), (0, 2, 3, 1))  6.09 us
    all_to_all x1, starting transfers between devices, per_device(): back = lax.all_to_all(values, axes, split_axis=0, concat_axis=0, tiled=True)  5.58 us
  transfers between devices with their start and end apart: 4, of which 0 were waited for; matrix products, arithmetic and copies ran while one was open for 32% of the time, Pallas kernels for 20%

profile of v2, /device:TPU:0, one launch (start us, length us, event | category | flops | bytes accessed | tf_op | source)
XLA Modules:
  0.0 195.4 jit_solution(9480438822425706488)
XLA Ops:
  0.6 1.0 copy.47
  1.7 5.2 %copy.48 = bf16[64,32,512]{0,2,1:T(8,128)(2,1)} copy(bf16[64,32,512]{2,1,0:T(8,128)(2,1)} %param.11) | data formatting | bytes 4194304 | tf_op args[0]
  6.9 2.5 %broadcast_multiply_fusion = bf16[64,32,512]{0,2,1:T(8,128)(2,1)S(1)} fusion(bf16[64,32,512]{0,2,1:T(8,128)(2,1)} %copy.48, bf16[64,512]{0,1:T(8,128)(2,1)S(1)} %convert_element_type.25), kind=kLoop, calls=%fused_computation.1 | loop fusion | flops 1048576 | bytes 4259840 | tf_op jit(solution)/shard_map/mul | solution.py:320
  9.4 1.2 pad_bitcast_fusion
  10.6 4.9 %copy.49 = bf16[65,64,8,32]{0,3,2,1:T(8,128)(2,1)S(1)} copy(bf16[65,64,8,32]{0,2,1,3:T(8,128)(2,1)S(1)} %pad_bitcast_fusion) | data formatting | bytes 4259840 | tf_op jit(solution)/shard_map/transpose | solution.py:322
  15.5 1.9 copy-done
  18.5 3.1 %collective-permute-start = (bf16[65,8,256]{2,1,0:T(8,128)(2,1)}, bf16[65,8,256]{2,1,0:T(8,128)(2,1)}, u32[]{:S(2)}, u32[]{:S(2)}) collective-permute-start(bf16[65,8,256]{2,1,0:T(8,128)(2,1)} %bitcast.3), channel_id=1, source_target_pairs={{0,1},{1,2},{2,3},{3,4},{4,5},{5,6},{6,7},{7,8},{8,9},{9,10},{10,1... | collective-permute-start | bytes 798728 | tf_op jit(solution)/shard_map/ppermute | solution.py:18
  22.6 1.3 collective-permute-start.1
  23.9 10.5 %dispatch.1 = (f32[32,4,512]{2,1,0:T(4,128)}, s32[1,8192]{1,0:T(1,128)}) custom-call(s32[1,8192]{1,0:T(1,128)} %bitcast.48, s32[1,8192]{1,0:T(1,128)} %bitcast.51, f32[3,8192]{1,0:T(4,128)} %frac_ref.1), custom_call_target="tpu_custom_call" | custom-call | tf_op jit(solution)/shard_map/dispatch/pallas_call | solution.py:197
  34.3 8.8 %all-to-all-start = ((f32[32,4,512]{2,1,0:T(4,128)}), f32[32,4,512]{2,1,0:T(4,128)}, u32[]{:S(2)}, u32[]{:S(2)}) async-start(f32[32,4,512]{2,1,0:T(4,128)} %get-tuple-element.5), calls=%async_computation | async-start | bytes 524288 | tf_op jit(solution)/shard_map/all_to_all | solution.py:319
  43.2 5.3 %copy.50 = bf16[65,8,8,256]{3,2,1,0:T(8,128)(2,1)S(1)} copy(bf16[65,8,8,256]{0,3,2,1:T(8,128)(2,1)} %bitcast.41) | data formatting | bytes 4259840 | tf_op jit(solution)/shard_map/reshape | solution.py:322
  49.4 1.9 pad_slice_fusion
  53.1 1.8 stack_reshape.25
  54.8 1.8 stack_reshape.26
  56.6 1.8 stack_reshape.27
  58.3 1.8 stack_reshape.28
  60.1 1.7 stack_reshape.29
  61.8 1.8 stack_reshape.30
  63.6 1.7 stack_reshape.31
  70.1 1.2 constant_dynamic-update-slice_fusion.10
  73.0 2.5 %convert_element_type.26.own_ref = f32[65,8,8,256]{3,2,1,0:T(8,128)} convert(bf16[65,8,8,256]{3,2,1,0:T(8,128)(2,1)S(1)} %copy.50) | non-fusion elementwise | flops 1064960 | bytes 6389760 | tf_op jit(solution)/shard_map/convert_element_type | solution.py:327
  76.7 2.6 %broadcast_in_dim.32 = bf16[64,64,8,32]{1,3,2,0:T(8,128)(2,1)} broadcast(bf16[64,64,8]{1,2,0:T(8,128)(2,1)S(1)} %copy.53), dimensions={0,1,2} | broadcast | bytes 2162688 | tf_op jit(solution)/shard_map/broadcast_in_dim | solution.py:125
  79.3 4.8 %copy.56.occ_ref = bf16[64,64,256]{2,1,0:T(8,128)(2,1)} copy(bf16[64,64,256]{1,2,0:T(8,128)(2,1)} %bitcast.43) | data formatting | bytes 4194304 | tf_op jit(solution)/shard_map/reshape | solution.py:125
  88.2 1.8 convert_element_type.27.prev_ref
  90.0 1.8 convert_element_type.28.next_ref
  91.8 27.7 %conv_block.1.blocks_ref = f32[64,8,8,256]{3,2,1,0:T(8,128)} custom-call(s32[1728]{0:T(1024)} %reshape.53.nb_ref, f32[65,8,8,256]{3,2,1,0:T(8,128)} %convert_element_type.26.own_ref, f32[65,8,256]{2,1,0:T(8,128)} %convert_element_type.27.prev_ref, f32[65,8,256]{2,1,0:T(8,128)} %convert_element_type.28.next_ref, bf16[64,64,256]{2,1,0:T(8,128)(2,1)} %copy.56.occ_ref, ...), custom_call_target="tpu_custom_call" | custom-call | flops 8000000000 | bytes 12582912 | tf_op jit(solution)/shard_map/conv_block/pallas_call | solution.py:126
  119.5 51.2 %sample_points.1 = f32[32,1,512]{2,1,0:T(1,128)} custom-call(f32[64,8,8,256]{3,2,1,0:T(8,128)} %conv_block.1.blocks_ref, f32[32,4,512]{2,1,0:T(4,128)} %all-to-all-done.recv_ref, bf16[64,32]{1,0:T(8,128)(2,1)} %copy.59.din_ref, f32[64,1]{1,0:T(8,128)} %copy.60.bias_ref, f32[64,1]{1,0:T(8,128)} %copy.61.dout_ref), custom_call_target="tpu_custom_call" | custom-call | tf_op jit(solution)/shard_map/sample_points/pallas_call | solution.py:252
  170.7 5.6 %all-to-all-start.1 = ((f32[32,1,512]{2,1,0:T(1,128)}), f32[32,1,512]{2,1,0:T(1,128)S(1)}, u32[]{:S(2)}, u32[]{:S(2)}) async-start(f32[32,1,512]{2,1,0:T(1,128)} %sample_points.1), calls=%async_computation.1 | async-start | bytes 131072 | tf_op jit(solution)/shard_map/all_to_all | solution.py:339
  176.3 2.5 %convert_element_type.30 = bf16[64,8,8,256]{3,2,1,0:T(8,128)(2,1)S(1)} convert(f32[64,8,8,256]{3,2,1,0:T(8,128)} %conv_block.1.blocks_ref) | non-fusion elementwise | flops 1048576 | bytes 6291456 | tf_op jit(solution)/shard_map/convert_element_type | solution.py:336
  178.8 3.8 %copy.57 = bf16[64,8,8,256]{0,3,2,1:T(8,128)(2,1)} copy(bf16[64,8,8,256]{3,2,1,0:T(8,128)(2,1)S(1)} %convert_element_type.30) | data formatting | bytes 4194304 | tf_op jit(solution)/shard_map/convert_element_type | solution.py:336
  182.6 6.8 %copy.62 = bf16[64,32,512]{2,1,0:T(8,128)(2,1)} copy(bf16[64,32,512]{0,1,2:T(8,128)(2,1)} %bitcast.42) | data formatting | bytes 4194304
  190.1 5.4 %collect.1 = f32[1,8192]{1,0:T(1,128)} custom-call(s32[1,8192]{1,0:T(1,128)} %bitcast.49, s32[1,8192]{1,0:T(1,128)} %get-tuple-element.4.slot_ref, f32[32,512]{1,0:T(8,128)} %bitcast.46), custom_call_target="tpu_custom_call" | custom-call | tf_op jit(solution)/shard_map/collect/pallas_call | solution.py:292
  (64 shorter events, 17.0 us)
Async XLA Ops:
  15.5 2.0 copy-start
  18.5 69.7 %collective-permute-start = (bf16[65,8,256]{2,1,0:T(8,128)(2,1)}, bf16[65,8,256]{2,1,0:T(8,128)(2,1)}, u32[]{:S(2)}, u32[]{:S(2)}) collective-permute-start(bf16[65,8,256]{2,1,0:T(8,128)(2,1)} %bitcast.3), channel_id=1, source_target_pairs={{0,1},{1,2},{2,3},{3,4},{4,5},{5,6},{6,7},{7,8},{8,9},{9,10},{10,1... | collective-permute-start | bytes 798728 | tf_op jit(solution)/shard_map/ppermute | solution.py:18
  22.6 67.4 %collective-permute-start.1 = (bf16[65,8,256]{2,1,0:T(8,128)(2,1)}, bf16[65,8,256]{2,1,0:T(8,128)(2,1)}, u32[]{:S(2)}, u32[]{:S(2)}) collective-permute-start(bf16[65,8,256]{2,1,0:T(8,128)(2,1)} %bitcast.4), channel_id=1, source_target_pairs={{1,0},{2,1},{3,2},{4,3},{5,4},{6,5},{7,6},{8,7},{9,8},{10,9},{11,1... | collective-permute-start | bytes 798728 | tf_op jit(solution)/shard_map/ppermute | solution.py:18
  34.3 85.2 %all-to-all-start = ((f32[32,4,512]{2,1,0:T(4,128)}), f32[32,4,512]{2,1,0:T(4,128)}, u32[]{:S(2)}, u32[]{:S(2)}) async-start(f32[32,4,512]{2,1,0:T(4,128)} %get-tuple-element.5), calls=%async_computation | async-start | bytes 524288 | tf_op jit(solution)/shard_map/all_to_all | solution.py:319
  43.2 6.0 %copy-start.5 = (bf16[32,32,3,3,3]{1,0,4,3,2:T(8,128)(2,1)S(1)}, bf16[32,32,3,3,3]{1,0,4,3,2:T(8,128)(2,1)}, u32[]{:S(2)}) copy-start(bf16[32,32,3,3,3]{1,0,4,3,2:T(8,128)(2,1)} %param.14) | copy-start | bytes 165892
  65.3 4.7 %copy-start.3 = (bf16[3,1,32,768]{3,2,0,1:T(8,128)(2,1)S(1)}, bf16[3,1,32,768]{3,2,0,1:T(8,128)(2,1)}, u32[]{:S(2)}) copy-start(bf16[3,1,32,768]{3,2,0,1:T(8,128)(2,1)} %stack_reshape.30) | copy-start | bytes 442372
  65.3 4.7 %copy-start.2 = (bf16[3,1,32,768]{3,2,0,1:T(8,128)(2,1)S(1)}, bf16[3,1,32,768]{3,2,0,1:T(8,128)(2,1)}, u32[]{:S(2)}) copy-start(bf16[3,1,32,768]{3,2,0,1:T(8,128)(2,1)} %stack_reshape.31) | copy-start | bytes 442372
  70.1 1.2 copy-start.1
  73.0 2.7 %copy-start.6 = (s32[64,27]{0,1:T(8,128)S(1)}, s32[64,27]{0,1:T(8,128)}, u32[]{:S(2)}) copy-start(s32[64,27]{0,1:T(8,128)} %param.13) | copy-start | bytes 20740
  73.0 3.6 %copy-start.4 = (bf16[64,64,8]{0,2,1:T(8,128)(2,1)S(1)}, bf16[64,64,8]{0,2,1:T(8,128)(2,1)}, u32[]{:S(2)}) copy-start(bf16[64,64,8]{0,2,1:T(8,128)(2,1)} %convert_bitcast_fusion) | copy-start | bytes 196612
  79.3 4.8 %copy-start.9 = (f32[32]{0:T(128)S(1)}, f32[32]{0:T(128)}, u32[]{:S(2)}) copy-start(f32[32]{0:T(128)} %param.15) | copy-start | bytes 388
  79.3 5.5 %copy-start.10 = (bf16[64]{0:T(256)(128)(2,1)S(1)}, bf16[64]{0:T(256)(128)(2,1)}, u32[]{:S(2)}) copy-start(bf16[64]{0:T(256)(128)(2,1)} %param.21) | copy-start | bytes 388
  79.3 6.2 %copy-start.8 = (f32[64]{0:T(128)S(1)}, f32[64]{0:T(128)}, u32[]{:S(2)}) copy-start(f32[64]{0:T(128)} %param.20) | copy-start | bytes 772
  79.3 6.9 %copy-start.7 = (bf16[64,32]{0,1:T(8,128)(2,1)S(1)}, bf16[64,32]{0,1:T(8,128)(2,1)}, u32[]{:S(2)}) copy-start(bf16[64,32]{0,1:T(8,128)(2,1)} %param.19) | copy-start | bytes 12292
  170.7 18.7 %all-to-all-start.1 = ((f32[32,1,512]{2,1,0:T(1,128)}), f32[32,1,512]{2,1,0:T(1,128)S(1)}, u32[]{:S(2)}, u32[]{:S(2)}) async-start(f32[32,1,512]{2,1,0:T(1,128)} %sample_points.1), calls=%async_computation.1 | async-start | bytes 131072 | tf_op jit(solution)/shard_map/all_to_all | solution.py:339
